TPU v7x, 256 devices: a whole 4x4x8 slice. The times are simulated.
256 devices in a mesh: chan: 32 (over z_lo, y, x), inp: 8 (over z_hi, core).
Axes of the slice: x: 4, y: 4, z: 8 (z_hi: 4, z_lo: 2; z = z_hi * 2 + z_lo), core: 2. Of those that a mesh axis runs over, the one named last changes fastest.
Arguments:
- voltages: bfloat16 [1024, 530432], P(('chan', 'inp')), may hold values from -6 to 6
Outputs:
- visibility: float32 [512, 1024, 1024], P(('chan', 'inp'))
All inputs are finite; a program needn't handle non-finite values.
Results may differ from a plain program's by a relative error of at most 0.0057.
Values may be sent and summed in bfloat16 or wider, within the bound.
A program may use at most 64 MiB of HBM per device.

v0:
```python
import jax
import jax.numpy as jnp
from jax import lax
from jax.sharding import PartitionSpec as P

FFT_LEN = 2048
CHAN_DEV = 2
NUM_TAPS = 4
SPECTRA = 256


def make_window():
    index = jnp.arange(NUM_TAPS * FFT_LEN, dtype=jnp.float32)
    shifted = (index + 0.5) / FFT_LEN - NUM_TAPS / 2.0
    taper = 0.54 - 0.46 * jnp.cos(2.0 * jnp.pi * (index + 0.5) / (NUM_TAPS * FFT_LEN))
    return (jnp.sinc(shifted) * taper).reshape(NUM_TAPS, FFT_LEN)


def make_table(channel_total):
    points = jnp.arange(FFT_LEN, dtype=jnp.int32)[:, None]
    bins = jnp.arange(channel_total, dtype=jnp.int32)[None, :] + FFT_LEN // 8
    phase = (points * bins % FFT_LEN).astype(jnp.float32) * (2.0 * jnp.pi / FFT_LEN)
    norm = 1.0 / jnp.sqrt(jnp.float32(FFT_LEN))
    return jnp.concatenate([jnp.cos(phase) * norm, -jnp.sin(phase) * norm], axis=1).astype(
        jnp.bfloat16
    )


def pair_products(left_re, left_im, right_re, right_im):
    real_part = jnp.einsum("cas,cbs->cab", left_re, right_re, preferred_element_type=jnp.float32)
    real_part = real_part + jnp.einsum(
        "cas,cbs->cab", left_im, right_im, preferred_element_type=jnp.float32
    )
    imag_part = jnp.einsum("cas,cbs->cab", left_im, right_re, preferred_element_type=jnp.float32)
    imag_part = imag_part - jnp.einsum(
        "cas,cbs->cab", left_re, right_im, preferred_element_type=jnp.float32
    )
    return (real_part, imag_part)


def local(voltages):
    local_inputs = voltages.shape[0]
    chan_count = lax.axis_size("chan")
    inp_count = lax.axis_size("inp")
    per_device = CHAN_DEV
    channel_total = per_device * chan_count * inp_count
    all_inputs = local_inputs * chan_count * inp_count
    window = make_window()
    frames = voltages.reshape(local_inputs, SPECTRA + NUM_TAPS - 1, FFT_LEN)
    filtered = jnp.zeros((local_inputs, SPECTRA, FFT_LEN), jnp.float32)
    for tap in range(NUM_TAPS):
        filtered = (
            filtered
            + frames[:, tap : tap + SPECTRA, :].astype(jnp.float32) * window[tap][None, None, :]
        )
    filtered = filtered.astype(jnp.bfloat16).reshape(local_inputs * SPECTRA, FFT_LEN)
    table = make_table(channel_total)
    spectra = lax.dot_general(
        table, filtered, (((0,), (1,)), ((), ())), preferred_element_type=jnp.float32
    )
    spectra = spectra.astype(jnp.bfloat16).reshape(
        2, chan_count, inp_count, per_device, local_inputs, SPECTRA
    )
    turned = lax.all_to_all(spectra, "chan", split_axis=1, concat_axis=1, tiled=True)
    turned = lax.all_to_all(turned, "inp", split_axis=2, concat_axis=2, tiled=True)
    turned = jnp.transpose(turned, (0, 3, 1, 2, 4, 5)).reshape(2, per_device, all_inputs, SPECTRA)
    real_in = turned[0]
    imag_in = turned[1]
    scale = 1.0 / SPECTRA
    real_part, imag_part = pair_products(real_in, imag_in, real_in, imag_in)
    rows = jnp.arange(all_inputs, dtype=jnp.int32)[:, None]
    cols = jnp.arange(all_inputs, dtype=jnp.int32)[None, :]
    return jnp.where((rows <= cols)[None], real_part, imag_part) * scale


def solution(mesh):
    in_specs = (P(("chan", "inp"), None),)
    out_specs = P(("chan", "inp"), None, None)
    return jax.shard_map(local, mesh=mesh, in_specs=in_specs, out_specs=out_specs, check_vma=False)
```

profile of v0, /device:TPU:33, one launch (start us, length us, event | category | flops | bytes accessed | tf_op | source)
XLA Modules:
  0.0 169.5 jit_solution(6760157225212179424)
XLA Ops:
  0.0 0.2 fusion.17
  0.2 18.3 %multiply_convert_fusion.1 = (bf16[2048,512]{1,0:T(8,128)(2,1)S(1)}, bf16[2048,512]{1,0:T(8,128)(2,1)}) fusion(s32[512]{0:T(512)S(1)} %iota_add_fusion), kind=kLoop, calls=%fused_computation.13 | loop fusion | flops 19922944 | bytes 4196352 | tf_op jit(solution)/shard_map/convert
  18.5 6.9 %reshape.44 = bf16[4,259,2048]{2,1,0:T(8,128)(2,1)} reshape(bf16[4,530432]{1,0:T(4,128)(2,1)} %param.1) | data formatting | bytes 8486912 | tf_op jit(solution)/shard_map/reshape | solution.py:49
  25.3 0.0 copy-start
  25.3 9.9 %add_convert_fusion = bf16[4,256,2048]{2,1,0:T(8,128)(2,1)S(1)} fusion(bf16[4,259,2048]{2,1,0:T(8,128)(2,1)} %reshape.44, f32[2048]{0:T(1024)S(1)} %get-tuple-element.8, f32[2048]{0:T(1024)S(1)} %get-tuple-element.9, f32[2048]{0:T(1024)S(1)} %get-tuple-element.10, f32[2048]{0:T(1024)S(1)} %get-tuple-element.7), kind=kLoop, calls=%fused_computation.1 | loop fusion | flops 25165824 | bytes 21004288 | tf_op jit(solution)/shard_map/convert_element_type | solution.py:56
  35.3 0.0 copy-done
  35.3 5.7 %fusion.10 = bf16[1024,1024]{1,0:T(8,128)(2,1)} fusion(bf16[1024,2048]{1,0:T(8,128)(2,1)S(1)} %bitcast.12, bf16[2048,512]{1,0:T(8,128)(2,1)S(1)} %copy-done, bf16[2048,512]{1,0:T(8,128)(2,1)S(1)} %get-tuple-element.11), kind=kOutput, calls=%fused_computation.18 | convolution fusion | flops 4304404480 | bytes 10485760 | tf_op jit(solution)/shard_map/dot_general | solution.py:58
  41.0 3.3 %reshape.46 = bf16[2,32,8,2,4,256]{5,4,3,2,1,0:T(4,128)(2,1)S(1)} reshape(bf16[1024,1024]{1,0:T(8,128)(2,1)} %fusion.10) | data formatting | bytes 4194304 | tf_op jit(solution)/shard_map/reshape | solution.py:61
  44.4 1.6 copy.6
  45.9 34.0 %all_to_all.10 = bf16[2,32,8,2,4,256]{5,4,3,2,0,1:T(4,128)(2,1)S(1)} all-to-all(bf16[2,32,8,2,4,256]{5,4,3,2,0,1:T(4,128)(2,1)S(1)} %copy.6), channel_id=1, replica_groups=mesh['chan'=32,'inp'=8] {'chan'}, dimensions={1} | all-to-all | bytes 4194304 | tf_op jit(solution)/shard_map/all_to_all | solution.py:64
  79.9 2.3 %copy.7 = bf16[2,32,8,2,4,256]{5,4,3,1,0,2:T(4,128)(2,1)} copy(bf16[2,32,8,2,4,256]{5,4,3,2,0,1:T(4,128)(2,1)S(1)} %all_to_all.10) | data formatting | bytes 4194304 | tf_op jit(solution)/shard_map/all_to_all | solution.py:64
  82.3 10.1 %all-to-all-start.1 = ((bf16[2,32,8,2,4,256]{5,4,3,1,0,2:T(4,128)(2,1)}), bf16[2,32,8,2,4,256]{5,4,3,1,0,2:T(4,128)(2,1)S(1)}, u32[]{:S(2)}, u32[]{:S(2)}) async-start(bf16[2,32,8,2,4,256]{5,4,3,1,0,2:T(4,128)(2,1)} %copy.7), calls=%async_computation.1 | async-start | bytes 4194304 | tf_op jit(solution)/shard_map/all_to_all | solution.py:65
  92.3 0.3 iota_compare_fusion
  92.6 50.2 %all-to-all-done.1 = bf16[2,32,8,2,4,256]{5,4,3,1,0,2:T(4,128)(2,1)S(1)} async-done(((bf16[2,32,8,2,4,256]{5,4,3,1,0,2:T(4,128)(2,1)}), bf16[2,32,8,2,4,256]{5,4,3,1,0,2:T(4,128)(2,1)S(1)}, u32[]{:S(2)}, u32[]{:S(2)}) %all-to-all-start.1) | async-done | bytes 2097184 | tf_op jit(solution)/shard_map/all_to_all | solution.py:65
  142.8 1.7 fusion.27
  144.5 0.6 copy.8
  145.1 0.3 squeeze.6
  145.4 2.8 %copy.9 = bf16[1,2,32,8,4,256]{5,4,3,2,1,0:T(4,128)(2,1)} copy(bf16[1,2,32,8,4,256]{5,4,1,2,0,3:T(4,128)(2,1)} %get-tuple-element.6) | data formatting | bytes 2097152 | tf_op jit(solution)/shard_map/slice | solution.py:68
  148.2 1.3 squeeze.7
  149.5 1.3 fusion.30
  150.8 4.7 %fusion.31 = f32[2,1024,1024]{2,1,0:T(8,128)} fusion(bf16[2,1024,256]{2,1,0:T(8,128)(2,1)S(1)} %squeeze.7, bf16[2,1024,256]{2,1,0:T(8,128)(2,1)S(1)} %squeeze.6), kind=kOutput, calls=%fused_computation.49 | convolution fusion | flops 1073741824 | bytes 10485760 | tf_op jit(solution)/shard_map/cas,cbs->cab/dot_general | solution.py:34
  155.5 4.5 %fusion.29 = f32[2,1024,1024]{2,1,0:T(8,128)} fusion(bf16[2,1024,256]{2,1,0:T(8,128)(2,1)S(1)} %squeeze.6), kind=kOutput, calls=%fused_computation.47 | convolution fusion | flops 1073741824 | bytes 9437184 | tf_op jit(solution)/shard_map/cas,cbs->cab/dot_general | solution.py:30
  160.0 9.5 %select_multiply_fusion = f32[2,1024,1024]{2,1,0:T(8,128)} fusion(f32[2,1024,1024]{2,1,0:T(8,128)} %fusion.31, f32[2,1024,1024]{2,1,0:T(8,128)} %fusion.29, f32[2,1024,1024]{2,1,0:T(8,128)S(1)} %fusion.30, pred[1024,1024]{1,0:T(8,128)(4,1)S(1)} %iota_compare_fusion, bf16[2,1024,256]{2,1,0:T(8,128)(2,1)S(1)} %squeeze.6, bf16[2,1024,256]{2,1,0:T(8,128)(2,1)S(1)} %squeeze.7), kind=kOutput, calls=%fused_computation | convolution fusion | flops 1082130432 | bytes 36700160 | tf_op jit(solution)/shard_map/cas,cbs->cab/dot_general | solution.py:35
  (2 shorter events, 0.0 us)
Async XLA Ops:
  25.3 9.9 %copy-start = (bf16[2048,512]{1,0:T(8,128)(2,1)S(1)}, bf16[2048,512]{1,0:T(8,128)(2,1)}, u32[]{:S(2)}) copy-start(bf16[2048,512]{1,0:T(8,128)(2,1)} %get-tuple-element.12) | copy-start | bytes 6291460
  82.3 60.6 %all-to-all-start.1 = ((bf16[2,32,8,2,4,256]{5,4,3,1,0,2:T(4,128)(2,1)}), bf16[2,32,8,2,4,256]{5,4,3,1,0,2:T(4,128)(2,1)S(1)}, u32[]{:S(2)}, u32[]{:S(2)}) async-start(bf16[2,32,8,2,4,256]{5,4,3,1,0,2:T(4,128)(2,1)} %copy.7), calls=%async_computation.1 | async-start | bytes 4194304 | tf_op jit(solution)/shard_map/all_to_all | solution.py:65
where the time goes:
time: 170 us; the launch traced here: 169 us
  waiting for transfers between devices  50.2 us (30%)
  blocking collectives  34 us (20%)
  other arithmetic  28.7 us (17%)
  matrix products  25.7 us (15%)
  local copies, waits for them, and re-layouts  20.7 us (12%)
  starting transfers between devices  10.1 us (6%)
    all_to_all x1, waiting for transfers between devices, local(): lax.all_to_all(turned, 'inp', split_axis=2, concat_axis=2, tiled=True)  50.2 us
    all_to_all x1, blocking collectives, local(): lax.all_to_all(spectra, 'chan', split_axis=1, concat_axis=1, tiled=True)  34 us
    another operation x1, other arithmetic  18.3 us
    all_to_all x1, starting transfers between devices, local(): lax.all_to_all(turned, 'inp', split_axis=2, concat_axis=2, tiled=True)  10.1 us
    convert_element_type x1, other arithmetic, local(): filtered.astype(jnp.bfloat16).reshape(local_inputs * SPECTRA, FFT_LEN)  9.94 us
    dot_general x1, matrix products, pair_products(): jnp.einsum('cas,cbs->cab', left_re, right_im, preferred_element_type=jnp....  9.46 us
    reshape x1, local copies, waits for them, and re-layouts, local(): frames = voltages.reshape(local_inputs, SPECTRA + NUM_TAPS - 1, FFT_LEN)  6.85 us
    dot_general x1, matrix products, local(): lax.dot_general(table, filtered, (((0,), (1,)), ((), ())), preferred_elem...  5.74 us
  transfers between devices with their start and end apart: 1, of which 1 were waited for; matrix products, arithmetic and copies ran while one was open for 0% of the time, Pallas kernels for 0%

commit v1 on v0

--- a/solution.py
+++ b/solution.py
@@ -1,12 +1,16 @@
 import jax
 import jax.numpy as jnp
 from jax import lax
+from jax.experimental import pallas as pl
+from jax.experimental.pallas import tpu as pltpu
 from jax.sharding import PartitionSpec as P
 
 FFT_LEN = 2048
 CHAN_DEV = 2
 NUM_TAPS = 4
 SPECTRA = 256
+DEVICES = 256
+MESH = pl.DeviceIdType.MESH
 
 
 def make_window():
@@ -26,6 +30,62 @@
     )
 
 
+def partner(step):
+    chan, inp = lax.axis_index("chan"), lax.axis_index("inp")
+    x, y, z, core = chan % 4, chan // 4 % 4, inp // 2 * 2 + chan // 16, inp % 2
+    core = (core + step % 2) % 2
+    z = (z + step // 2 % 8) % 8
+    x = (x + step // 16 % 4) % 4
+    y = (y + step // 64) % 4
+    return z % 2 * 16 + y * 4 + x, z // 2 * 2 + core
+
+
+def exchange_kernel(send_ref, recv_ref, own_sem, send_sem, recv_sem):
+    me = lax.axis_index("chan") * 8 + lax.axis_index("inp")
+    barrier = pltpu.get_barrier_semaphore()
+
+    def greet(step, carry):
+        pl.semaphore_signal(barrier, inc=1, device_id=partner(step), device_id_type=MESH)
+        return carry
+
+    lax.fori_loop(1, DEVICES, greet, 0)
+    own = pltpu.make_async_copy(send_ref.at[me], recv_ref.at[me], own_sem)
+    own.start()
+    pl.semaphore_wait(barrier, DEVICES - 1)
+
+    def send(step, carry):
+        chan, inp = partner(step)
+        pltpu.make_async_remote_copy(
+            src_ref=send_ref.at[chan * 8 + inp],
+            dst_ref=recv_ref.at[me],
+            send_sem=send_sem,
+            recv_sem=recv_sem,
+            device_id=(chan, inp),
+            device_id_type=MESH,
+        ).start()
+        return carry
+
+    lax.fori_loop(1, DEVICES, send, 0)
+    own.wait()
+    all_but_own = pl.ds(0, DEVICES - 1)
+    pltpu.make_async_copy(send_ref.at[all_but_own], recv_ref.at[all_but_own], send_sem).wait()
+    pltpu.make_async_copy(send_ref.at[all_but_own], recv_ref.at[all_but_own], recv_sem).wait()
+
+
+def exchange(blocks):
+    return pl.pallas_call(
+        exchange_kernel,
+        out_shape=jax.ShapeDtypeStruct(blocks.shape, blocks.dtype),
+        in_specs=[pl.BlockSpec(memory_space=pltpu.VMEM)],
+        out_specs=pl.BlockSpec(memory_space=pltpu.VMEM),
+        scratch_shapes=[pltpu.SemaphoreType.DMA] * 3,
+        compiler_params=pltpu.CompilerParams(
+            collective_id=0, has_side_effects=True, vmem_limit_bytes=16 << 20
+        ),
+        name="exchange",
+    )(blocks)
+
+
 def pair_products(left_re, left_im, right_re, right_im):
     real_part = jnp.einsum("cas,cbs->cab", left_re, right_re, preferred_element_type=jnp.float32)
     real_part = real_part + jnp.einsum(
@@ -40,11 +100,8 @@
 
 def local(voltages):
     local_inputs = voltages.shape[0]
-    chan_count = lax.axis_size("chan")
-    inp_count = lax.axis_size("inp")
-    per_device = CHAN_DEV
-    channel_total = per_device * chan_count * inp_count
-    all_inputs = local_inputs * chan_count * inp_count
+    channel_total = CHAN_DEV * DEVICES
+    all_inputs = local_inputs * DEVICES
     window = make_window()
     frames = voltages.reshape(local_inputs, SPECTRA + NUM_TAPS - 1, FFT_LEN)
     filtered = jnp.zeros((local_inputs, SPECTRA, FFT_LEN), jnp.float32)
@@ -58,12 +115,10 @@
     spectra = lax.dot_general(
         table, filtered, (((0,), (1,)), ((), ())), preferred_element_type=jnp.float32
     )
-    spectra = spectra.astype(jnp.bfloat16).reshape(
-        2, chan_count, inp_count, per_device, local_inputs, SPECTRA
-    )
-    turned = lax.all_to_all(spectra, "chan", split_axis=1, concat_axis=1, tiled=True)
-    turned = lax.all_to_all(turned, "inp", split_axis=2, concat_axis=2, tiled=True)
-    turned = jnp.transpose(turned, (0, 3, 1, 2, 4, 5)).reshape(2, per_device, all_inputs, SPECTRA)
+    spectra = spectra.astype(jnp.bfloat16).reshape(2, DEVICES, CHAN_DEV, local_inputs, SPECTRA)
+    blocks = jnp.transpose(spectra, (1, 0, 2, 3, 4)).reshape(DEVICES, 16, SPECTRA)
+    turned = exchange(blocks).reshape(DEVICES, 2, CHAN_DEV, local_inputs, SPECTRA)
+    turned = jnp.transpose(turned, (1, 2, 0, 3, 4)).reshape(2, CHAN_DEV, all_inputs, SPECTRA)
     real_in = turned[0]
     imag_in = turned[1]
     scale = 1.0 / SPECTRA

time: 170 us -> 155 us (0.912)
  Pallas kernels: 0 us -> 73.9 us
  waiting for transfers between devices: 50.2 us -> 0 us
  blocking collectives: 34 us -> 0 us
  starting transfers between devices: 10.1 us -> 0 us
  local copies, waits for them, and re-layouts: 20.7 us -> 25 us
    pallas_call x0 -> x1, Pallas kernels: none -> 73.9 us  [exchange(): pl.pallas_call(exchange_kernel, out_shape=jax.ShapeDtypeStruct(blocks.sha...]
    all_to_all x1 -> x0, waiting for transfers between devices: 50.2 us -> none  [local(): lax.all_to_all(turned, 'inp', split_axis=2, concat_axis=2, tiled=True)]
    all_to_all x1 -> x0, blocking collectives: 34 us -> none  [local(): lax.all_to_all(spectra, 'chan', split_axis=1, concat_axis=1, tiled=True)]
    all_to_all x1 -> x0, starting transfers between devices: 10.1 us -> none  [local(): lax.all_to_all(turned, 'inp', split_axis=2, concat_axis=2, tiled=True)]
    reshape x0 -> x2, local copies, waits for them, and re-layouts: none -> 5.09 us  [the longest x1 2.54 us: local(): exchange(blocks).reshape(DEVICES, 2, CHAN_DEV, local_inputs, SPECTRA)]
    dot_general x1, matrix products: 4.69 us -> 1.29 us  [pair_products(): jnp.einsum('cas,cbs->cab', left_im, right_re, preferred_element_type=jnp....]
    dot_general x1, matrix products: 1.28 us -> 4.51 us  [pair_products(): jnp.einsum('cas,cbs->cab', left_im, right_im, preferred_element_type=jnp....]
    all_to_all x1 -> x0, local copies, waits for them, and re-layouts: 2.33 us -> none  [local(): lax.all_to_all(spectra, 'chan', split_axis=1, concat_axis=1, tiled=True)]
  transfers between devices with their start and end apart: 1 -> 0, of which waited for: 1 -> 0; matrix products, arithmetic and copies ran while one was open for 0% -> 0% of each run, Pallas kernels for 0% -> 0%
where the time goes in v1:
time: 155 us; the launch traced here: 153 us
  Pallas kernels  73.9 us (48%)
  other arithmetic  28.7 us (19%)
  matrix products  25.7 us (17%)
  local copies, waits for them, and re-layouts  25 us (16%)
    pallas_call x1, Pallas kernels, exchange(): pl.pallas_call(exchange_kernel, out_shape=jax.ShapeDtypeStruct(blocks.sha...  73.9 us
    another operation x1, other arithmetic  18.3 us
    convert_element_type x1, other arithmetic, local(): filtered.astype(jnp.bfloat16).reshape(local_inputs * SPECTRA, FFT_LEN)  9.94 us
    dot_general x1, matrix products, pair_products(): jnp.einsum('cas,cbs->cab', left_re, right_im, preferred_element_type=jnp....  9.51 us
    reshape x1, local copies, waits for them, and re-layouts, local(): frames = voltages.reshape(local_inputs, SPECTRA + NUM_TAPS - 1, FFT_LEN)  6.85 us
    dot_general x1, matrix products, local(): lax.dot_general(table, filtered, (((0,), (1,)), ((), ())), preferred_elem...  5.74 us
    reshape x2, local copies, waits for them, and re-layouts, local(): spectra.astype(jnp.bfloat16)  5.37 us
    dot_general x1, matrix products, pair_products(): jnp.einsum('cas,cbs->cab', left_re, right_re, preferred_element_type=jnp....  4.69 us

profile of v1, /device:TPU:33, one launch (start us, length us, event | category | flops | bytes accessed | tf_op | source)
XLA Modules:
  0.0 153.4 jit_solution(15726568674087582689)
XLA Ops:
  0.0 0.2 fusion.17
  0.2 0.3 iota_compare_fusion
  0.5 18.3 %multiply_convert_fusion.1 = (bf16[2048,512]{1,0:T(8,128)(2,1)S(1)}, bf16[2048,512]{1,0:T(8,128)(2,1)}) fusion(s32[512]{0:T(512)S(1)} %iota_add_fusion), kind=kLoop, calls=%fused_computation.13 | loop fusion | flops 19922944 | bytes 4196352 | tf_op jit(solution)/shard_map/convert
  18.8 6.9 %reshape.50 = bf16[4,259,2048]{2,1,0:T(8,128)(2,1)} reshape(bf16[4,530432]{1,0:T(4,128)(2,1)} %param.1) | data formatting | bytes 8486912 | tf_op jit(solution)/shard_map/reshape | solution.py:106
  25.6 0.0 copy-start.1
  25.6 9.9 %add_convert_fusion = bf16[4,256,2048]{2,1,0:T(8,128)(2,1)S(1)} fusion(bf16[4,259,2048]{2,1,0:T(8,128)(2,1)} %reshape.50, f32[2048]{0:T(1024)S(1)} %get-tuple-element.8, f32[2048]{0:T(1024)S(1)} %get-tuple-element.9, f32[2048]{0:T(1024)S(1)} %get-tuple-element.10, f32[2048]{0:T(1024)S(1)} %get-tuple-element.7), kind=kLoop, calls=%fused_computation.1 | loop fusion | flops 25165824 | bytes 21004288 | tf_op jit(solution)/shard_map/convert_element_type | solution.py:113
  35.6 0.0 copy-done.1
  35.6 5.7 %fusion.10 = bf16[1024,1024]{1,0:T(8,128)(2,1)} fusion(bf16[1024,2048]{1,0:T(8,128)(2,1)S(1)} %bitcast.16, bf16[2048,512]{1,0:T(8,128)(2,1)S(1)} %copy-done.1, bf16[2048,512]{1,0:T(8,128)(2,1)S(1)} %get-tuple-element.11), kind=kOutput, calls=%fused_computation.19 | convolution fusion | flops 4304404480 | bytes 10485760 | tf_op jit(solution)/shard_map/dot_general | solution.py:115
  41.3 3.3 %reshape.52 = bf16[2,256,2,4,256]{4,3,2,1,0:T(4,128)(2,1)S(1)} reshape(bf16[1024,1024]{1,0:T(8,128)(2,1)} %fusion.10) | data formatting | bytes 4194304 | tf_op jit(solution)/shard_map/reshape | solution.py:118
  44.7 2.0 %copy.9 = bf16[2,256,2,4,256]{4,3,2,0,1:T(4,128)(2,1)} copy(bf16[2,256,2,4,256]{4,3,2,1,0:T(4,128)(2,1)S(1)} %reshape.52) | data formatting | bytes 4194304 | tf_op jit(solution)/shard_map/reshape | solution.py:118
  46.7 2.5 %reshape.53.send_ref = bf16[256,16,256]{2,1,0:T(8,128)(2,1)S(1)} reshape(bf16[256,2,2,4,256]{4,3,2,1,0:T(4,128)(2,1)} %bitcast.15) | data formatting | bytes 4194304 | tf_op jit(solution)/shard_map/reshape | solution.py:119
  49.3 73.9 %exchange.1 = bf16[256,16,256]{2,1,0:T(8,128)(2,1)S(1)} custom-call(bf16[256,16,256]{2,1,0:T(8,128)(2,1)S(1)} %reshape.53.send_ref), custom_call_target="tpu_custom_call" | custom-call | tf_op jit(solution)/shard_map/exchange/pallas_call | solution.py:76
  123.1 0.0 copy-start
  123.1 1.3 copy-done
  124.4 2.5 %reshape.54 = bf16[256,2,2,4,256]{4,3,2,1,0:T(4,128)(2,1)S(1)} reshape(bf16[256,16,256]{2,1,0:T(8,128)(2,1)} %copy-done) | data formatting | bytes 4194304 | tf_op jit(solution)/shard_map/reshape | solution.py:120
  127.0 1.7 %fusion.27 = (bf16[1,2,256,4,256]{4,3,1,0,2:T(4,128)(2,1)S(1)}, bf16[1,2,256,4,256]{4,3,1,0,2:T(4,128)(2,1)}) fusion(bf16[2,2,256,4,256]{4,3,1,0,2:T(4,128)(2,1)S(1)} %bitcast.14), kind=kLoop, calls=%fused_computation.46 | loop fusion | bytes 4194304 | tf_op jit(solution)/shard_map/slice | solution.py:122
  128.7 0.4 copy.6
  129.1 0.5 squeeze.6
  129.5 2.6 %copy.7 = bf16[1,2,256,4,256]{4,3,2,1,0:T(4,128)(2,1)} copy(bf16[1,2,256,4,256]{4,3,1,0,2:T(4,128)(2,1)} %get-tuple-element.6) | data formatting | bytes 2097152 | tf_op jit(solution)/shard_map/slice | solution.py:123
  132.1 1.3 squeeze.7
  133.4 1.3 fusion.31
  134.7 4.5 %fusion.30 = f32[2,1024,1024]{2,1,0:T(8,128)} fusion(bf16[2,1024,256]{2,1,0:T(8,128)(2,1)S(1)} %squeeze.7), kind=kOutput, calls=%fused_computation.49 | convolution fusion | flops 1073741824 | bytes 9437184 | tf_op jit(solution)/shard_map/cas,cbs->cab/dot_general | solution.py:91
  139.2 4.7 %fusion.29 = f32[2,1024,1024]{2,1,0:T(8,128)} fusion(bf16[2,1024,256]{2,1,0:T(8,128)(2,1)S(1)} %squeeze.6), kind=kOutput, calls=%fused_computation.48 | convolution fusion | flops 1073741824 | bytes 9437184 | tf_op jit(solution)/shard_map/cas,cbs->cab/dot_general | solution.py:90
  143.9 9.5 %select_multiply_fusion = f32[2,1024,1024]{2,1,0:T(8,128)} fusion(f32[2,1024,1024]{2,1,0:T(8,128)S(1)} %fusion.31, f32[2,1024,1024]{2,1,0:T(8,128)} %fusion.29, f32[2,1024,1024]{2,1,0:T(8,128)} %fusion.30, pred[1024,1024]{1,0:T(8,128)(4,1)S(1)} %iota_compare_fusion, bf16[2,1024,256]{2,1,0:T(8,128)(2,1)S(1)} %squeeze.6, bf16[2,1024,256]{2,1,0:T(8,128)(2,1)S(1)} %squeeze.7), kind=kOutput, calls=%fused_computation | convolution fusion | flops 1082130432 | bytes 36700160 | tf_op jit(solution)/shard_map/cas,cbs->cab/dot_general | solution.py:95
  (2 shorter events, 0.0 us)
Async XLA Ops:
  25.6 9.9 %copy-start.1 = (bf16[2048,512]{1,0:T(8,128)(2,1)S(1)}, bf16[2048,512]{1,0:T(8,128)(2,1)}, u32[]{:S(2)}) copy-start(bf16[2048,512]{1,0:T(8,128)(2,1)} %get-tuple-element.12) | copy-start | bytes 6291460
  123.1 1.3 copy-start

commit v2 on v0

v2 whole, which is shorter than its diff:
```python
import jax
import jax.numpy as jnp
import numpy as np
from jax import lax
from jax.experimental import pallas as pl
from jax.experimental.pallas import tpu as pltpu
from jax.sharding import PartitionSpec as P

FFT_LEN = 2048
CHANNELS = 512
NUM_TAPS = 4
SPECTRA = 256
FRAMES = SPECTRA + NUM_TAPS - 1
INPUTS = 1024
DEVICES = 256
HALF = SPECTRA // 2
MESH = pl.DeviceIdType.MESH


def make_window():
    index = np.arange(NUM_TAPS * FFT_LEN, dtype=np.float64) + 0.5
    shifted = index / FFT_LEN - NUM_TAPS / 2.0
    taper = 0.54 - 0.46 * np.cos(2.0 * np.pi * index / (NUM_TAPS * FFT_LEN))
    window = (np.sinc(shifted) * taper).astype(np.float32).reshape(NUM_TAPS, 16, 1, 128)
    return np.broadcast_to(window, (NUM_TAPS, 16, 4, 128)).reshape(NUM_TAPS, 64, 128)


def make_table():
    bins = np.arange(CHANNELS, dtype=np.int64)[:, None] + FFT_LEN // 8
    phase = (bins * np.arange(FFT_LEN, dtype=np.int64)[None, :] % FFT_LEN) * (2.0 * np.pi / FFT_LEN)
    both = np.stack([np.cos(phase), -np.sin(phase)]) / np.sqrt(FFT_LEN)
    both = both.reshape(2, 2, 4, 32, 2, FFT_LEN).transpose(2, 4, 0, 1, 3, 5)
    return both.reshape(4, 256, FFT_LEN).astype(np.float32).astype(jnp.bfloat16)


def coordinates():
    chan, inp = lax.axis_index("chan"), lax.axis_index("inp")
    return chan % 4, chan // 4 % 4, inp // 2 * 2 + chan // 16, inp % 2


def device_at(x, y, z, core):
    return z % 2 * 16 + y * 4 + x, z // 2 * 2 + core


def away(dx, dy, dz, dcore):
    x, y, z, core = coordinates()
    return device_at((x + dx) % 4, (y + dy) % 4, (z + dz) % 8, (core + dcore) % 2)


def spectra_kernel(
    volt_hbm, window_ref, table_hbm, out_ref,
    volt, table, filtered, send, recv, unpacked,
    volt_sems, table_sems, send_sem, recv_sems, met_sem,
):
    x, y, z, core = coordinates()
    me = (z % 2) * 128 + y * 32 + x * 8 + z // 2 * 2 + core
    barrier = pltpu.get_barrier_semaphore()

    cuts = ((0, 66), (66, 65), (131, 64), (195, 64))
    volt_copies = [
        pltpu.make_async_copy(volt_hbm.at[pl.ds(at, n)], volt.at[pl.ds(at, n)], volt_sems.at[i])
        for i, (at, n) in enumerate(cuts)
    ]
    table_copies = [
        pltpu.make_async_copy(table_hbm.at[(y + g) % 4], table.at[g], table_sems.at[g])
        for g in range(4)
    ]
    for copy in volt_copies[:2] + table_copies[:1] + volt_copies[2:] + table_copies[1:]:
        copy.start()

    def greet(step, carry):
        for target in (away(step % 4, step // 4, 0, 0), away(0, 0, step // 2, step % 2)):
            pl.semaphore_signal(barrier, inc=1, device_id=target, device_id_type=MESH)
        return carry

    lax.fori_loop(1, 16, greet, 0)

    def filter_half(half):
        for q in range(4):
            rows = slice(q * 16, (q + 1) * 16)
            taps = [window_ref[t, rows, :][None] for t in range(NUM_TAPS)]

            def block(i, carry):
                at = pl.multiple_of(half * HALF + i * 16, 16)
                frames = volt[pl.ds(at, 19), rows, :].astype(jnp.float32)
                total = frames[0:16] * taps[0]
                for t in range(1, NUM_TAPS):
                    total = total + frames[t : t + 16] * taps[t]
                total = jnp.transpose(total, (1, 0, 2)).astype(jnp.bfloat16)
                for r in range(16):
                    n, a = q * 4 + r // 4, r % 4
                    to = pl.multiple_of(half * 512 + a * HALF + i * 16, 16)
                    filtered[pl.ds(to, 16), n * 128 : (n + 1) * 128] = total[r]
                return carry

            lax.fori_loop(0, 8, block, 0)

    def transform(g, half):
        parts = []
        for pair in range(2):
            at = half * 512 + pair * 256
            product = lax.dot_general(
                table[g], filtered[at : at + 256, :], (((1,), (1,)), ((), ())),
                preferred_element_type=jnp.float32,
            )
            parts += [product[:, :128].reshape(4, 64, 128), product[:, 128:].reshape(4, 64, 128)]
        block = jnp.concatenate(parts, axis=0)
        send[g, :, half] = jnp.transpose(block, (1, 0, 2)).astype(jnp.bfloat16)

    def send_group(g, half, recv_sem):
        def one(step, carry):
            target = away(step // 16, g, step % 8, step // 8)
            slot = target[0] // 16 * 32 + target[0] % 4 * 8 + target[1]
            source, landing = send.at[g, slot], recv.at[me]
            if half is not None:
                source, landing = source.at[half], landing.at[half]
            pltpu.make_async_remote_copy(
                src_ref=source, dst_ref=landing, send_sem=send_sem, recv_sem=recv_sem,
                device_id=target, device_id_type=MESH,
            ).start()
            return carry

        lax.fori_loop(1 if g == 0 else 0, 64, one, 0)

    def unpack(g):
        for z_lo in range(2):
            first = z_lo * 128 + (y + 4 - g) % 4 * 32
            for half in range(2):
                got = recv[pl.ds(first, 32), half].astype(jnp.float32) * 0.0625
                unpacked[...] = got.reshape(512, 128)
                for comp in range(4):
                    part = unpacked[pl.ds(comp, 128, stride=4), :]
                    to = pl.ds(pl.multiple_of(first * 4, 128), 128)
                    lanes = comp % 2 * 256 + half * 128
                    out_ref[comp // 2, to, lanes : lanes + 128] = part.astype(jnp.bfloat16)
                    if comp % 2 == 0:
                        out_ref[comp // 2, to, 512 + lanes : 640 + lanes] = (-part).astype(jnp.bfloat16)

    for copy in volt_copies[:2]:
        copy.wait()
    filter_half(0)
    pl.semaphore_wait(barrier, 30)

    def meet(step, carry):
        target = away(0, 0, step // 2, step % 2)
        pl.semaphore_signal(met_sem, inc=1, device_id=target, device_id_type=MESH)
        return carry

    lax.fori_loop(1, 16, meet, 0)
    table_copies[0].wait()
    transform(0, 0)
    pl.semaphore_wait(met_sem, 15)
    send_group(0, 0, recv_sems.at[0])
    for copy in volt_copies[2:]:
        copy.wait()
    filter_half(1)
    transform(0, 1)
    send_group(0, 1, recv_sems.at[1])
    for g in range(1, 4):
        table_copies[g].wait()
        transform(g, 0)
        transform(g, 1)
        send_group(g, None, recv_sems.at[g + 1])
    recv[pl.ds(me, 1)] = send[0, pl.ds(z % 2 * 32 + x * 8 + z // 2 * 2 + core, 1)]

    near = recv.at[pl.ds(0, 63), 0]
    pltpu.make_async_copy(near, near, recv_sems.at[0]).wait()
    pltpu.make_async_copy(near, near, recv_sems.at[1]).wait()
    unpack(0)
    far = recv.at[pl.ds(0, 64)]
    for g in range(1, 4):
        pltpu.make_async_copy(far, far, recv_sems.at[g + 1]).wait()
        unpack(g)
    sent = recv.at[pl.ds(0, 255)]
    pltpu.make_async_copy(sent, sent, send_sem).wait()


def spectra_of(voltages, window, table):
    return pl.pallas_call(
        spectra_kernel,
        out_shape=jax.ShapeDtypeStruct((2, INPUTS, 768), jnp.bfloat16),
        in_specs=[
            pl.BlockSpec(memory_space=pltpu.HBM),
            pl.BlockSpec(memory_space=pltpu.VMEM),
            pl.BlockSpec(memory_space=pltpu.HBM),
        ],
        out_specs=pl.BlockSpec(memory_space=pltpu.VMEM),
        scratch_shapes=[
            pltpu.VMEM((FRAMES, 64, 128), jnp.bfloat16),
            pltpu.VMEM((4, 256, FFT_LEN), jnp.bfloat16),
            pltpu.VMEM((1024, FFT_LEN), jnp.bfloat16),
            pltpu.VMEM((4, 64, 2, 16, 128), jnp.bfloat16),
            pltpu.VMEM((DEVICES, 2, 16, 128), jnp.bfloat16),
            pltpu.VMEM((512, 128), jnp.float32),
            pltpu.SemaphoreType.DMA((4,)),
            pltpu.SemaphoreType.DMA((4,)),
            pltpu.SemaphoreType.DMA,
            pltpu.SemaphoreType.DMA((5,)),
            pltpu.SemaphoreType.REGULAR,
        ],
        compiler_params=pltpu.CompilerParams(
            collective_id=0, has_side_effects=True, vmem_limit_bytes=40 << 20
        ),
        name="spectra_exchange",
    )(voltages, window, table)


def gram_kernel(in_ref, out_ref):
    block = pl.program_id(0) % 4
    dims = (((1,), (1,)), ((), ()))
    for k in range(4):

        @pl.when(block == k)
        def _():
            rows = slice(k * 256, (k + 1) * 256)
            real = lax.dot_general(
                in_ref[0, rows, :512], in_ref[0, k * 256 :, :512], dims,
                preferred_element_type=jnp.float32,
            )
            imag = lax.dot_general(
                in_ref[0, rows, 256:], in_ref[0, : (k + 1) * 256, :512], dims,
                preferred_element_type=jnp.float32,
            )
            if k > 0:
                out_ref[0, :, : k * 256] = imag[:, : k * 256]
            down = lax.broadcasted_iota(jnp.int32, (256, 256), 0)
            across = lax.broadcasted_iota(jnp.int32, (256, 256), 1)
            out_ref[0, :, rows] = jnp.where(down <= across, real[:, :256], imag[:, k * 256 :])
            if k < 3:
                out_ref[0, :, (k + 1) * 256 :] = real[:, 256:]


def gram(spectra):
    return pl.pallas_call(
        gram_kernel,
        grid=(8,),
        out_shape=jax.ShapeDtypeStruct((2, INPUTS, INPUTS), jnp.float32),
        in_specs=[pl.BlockSpec((1, INPUTS, 768), lambda i: (i // 4, 0, 0))],
        out_specs=pl.BlockSpec((1, 256, INPUTS), lambda i: (i // 4, i % 4, 0)),
        compiler_params=pltpu.CompilerParams(vmem_limit_bytes=24 << 20),
        name="gram",
    )(spectra)


def local(voltages):
    tiles = voltages.reshape(4, FRAMES * 16, 128).transpose(1, 0, 2).reshape(FRAMES, 64, 128)
    return gram(spectra_of(tiles, jnp.asarray(make_window()), jnp.asarray(make_table())))


def solution(mesh):
    in_specs = (P(("chan", "inp"), None),)
    out_specs = P(("chan", "inp"), None, None)
    return jax.shard_map(local, mesh=mesh, in_specs=in_specs, out_specs=out_specs, check_vma=False)
```

time: 170 us -> 75.1 us (0.44)
  the two profiles are of different devices: /device:TPU:33 before, /device:TPU:1 now
where the time goes in v2:
time: 75.1 us; the launch traced here: 74.9 us
  Pallas kernels  69.6 us (93%)
  local copies, waits for them, and re-layouts  5.29 us (7%)
    pallas_call x1, Pallas kernels, spectra_of(): pl.pallas_call(spectra_kernel, out_shape=jax.ShapeDtypeStruct((2, INPUTS,...  62.9 us
    pallas_call x1, Pallas kernels, gram(): pl.pallas_call(gram_kernel, grid=(8,), out_shape=jax.ShapeDtypeStruct((2,...  6.7 us
    unnamed x6, local copies, waits for them, and re-layouts  5.29 us

profile of v2, /device:TPU:1, one launch (start us, length us, event | category | flops | bytes accessed | tf_op | source)
XLA Modules:
  0.0 74.9 jit_solution(11485347330545720468)
XLA Ops:
  0.0 0.0 copy-start
  0.0 2.2 %copy-done = bf16[4,530432]{1,0:T(4,128)(2,1)S(1)} copy-done((bf16[4,530432]{1,0:T(4,128)(2,1)S(1)}, bf16[4,530432]{1,0:T(4,128)(2,1)}, u32[]{:S(2)}) %copy-start) | copy-done | bytes 4243480
  2.2 0.0 copy-start.1
  2.2 2.2 %copy-done.1 = bf16[4,256,2048]{2,1,0:T(8,128)(2,1)S(1)} copy-done((bf16[4,256,2048]{2,1,0:T(8,128)(2,1)S(1)}, bf16[4,256,2048]{2,1,0:T(8,128)(2,1)}, u32[]{:S(2)}) %copy-start.1) | copy-done | bytes 4194328
  4.4 0.0 copy-start.2
  4.4 0.9 %copy-done.2 = f32[4,64,128]{2,1,0:T(8,128)S(1)} copy-done((f32[4,64,128]{2,1,0:T(8,128)S(1)}, f32[4,64,128]{2,1,0:T(8,128)}, u32[]{:S(2)}) %copy-start.2) | copy-done | bytes 131096
  5.3 62.9 %spectra_exchange.1.in_ref = bf16[2,1024,768]{2,1,0:T(8,128)(2,1)S(1)} custom-call(bf16[259,64,128]{2,1,0:T(8,128)(2,1)S(1)} %bitcast.5, f32[4,64,128]{2,1,0:T(8,128)S(1)} %copy-done.2, bf16[4,256,2048]{2,1,0:T(8,128)(2,1)S(1)} %copy-done.1), custom_call_target="tpu_custom_call" | custom-call | tf_op jit(solution)/shard_map/spectra_exchange/pallas_call | solution.py:179
  68.2 6.7 %gram.1 = f32[2,1024,1024]{2,1,0:T(8,128)} custom-call(bf16[2,1024,768]{2,1,0:T(8,128)(2,1)S(1)} %spectra_exchange.1.in_ref), custom_call_target="tpu_custom_call" | custom-call | tf_op jit(solution)/shard_map/gram/pallas_call | solution.py:234
Async XLA Ops:
  0.0 2.2 %copy-start = (bf16[4,530432]{1,0:T(4,128)(2,1)S(1)}, bf16[4,530432]{1,0:T(4,128)(2,1)}, u32[]{:S(2)}) copy-start(bf16[4,530432]{1,0:T(4,128)(2,1)} %param.3) | copy-start | bytes 12730372
  2.2 2.2 %copy-start.1 = (bf16[4,256,2048]{2,1,0:T(8,128)(2,1)S(1)}, bf16[4,256,2048]{2,1,0:T(8,128)(2,1)}, u32[]{:S(2)}) copy-start(bf16[4,256,2048]{2,1,0:T(8,128)(2,1)} %constant.5.clone.table_hbm) | copy-start | bytes 12582916
  4.4 0.9 %copy-start.2 = (f32[4,64,128]{2,1,0:T(8,128)S(1)}, f32[4,64,128]{2,1,0:T(8,128)}, u32[]{:S(2)}) copy-start(f32[4,64,128]{2,1,0:T(8,128)} %constant.4.clone.window_ref) | copy-start | bytes 393220

commit v3 on v2

v3 whole, which is shorter than its diff:
```python
import jax
import jax.numpy as jnp
import numpy as np
from jax import lax
from jax.experimental import pallas as pl
from jax.experimental.pallas import tpu as pltpu
from jax.sharding import PartitionSpec as P

FFT_LEN = 2048
CHANNELS = 512
NUM_TAPS = 4
SPECTRA = 256
FRAMES = SPECTRA + NUM_TAPS - 1
INPUTS = 1024
DEVICES = 256
HALF = SPECTRA // 2
PITCH = 17
WINDOW_PAD = 96
MESH = pl.DeviceIdType.MESH


def make_window():
    index = np.arange(NUM_TAPS * FFT_LEN, dtype=np.float64) + 0.5
    shifted = index / FFT_LEN - NUM_TAPS / 2.0
    taper = 0.54 - 0.46 * np.cos(2.0 * np.pi * index / (NUM_TAPS * FFT_LEN))
    window = (np.sinc(shifted) * taper).astype(np.float32).reshape(NUM_TAPS, 16, 1, 128)
    window = np.broadcast_to(window, (NUM_TAPS, 16, 4, 128)).reshape(NUM_TAPS, 64, 128)
    return np.concatenate([window, np.zeros((WINDOW_PAD - NUM_TAPS, 64, 128), np.float32)])


def make_table():
    bins = np.arange(CHANNELS, dtype=np.int64)[:, None] + FFT_LEN // 8
    phase = (bins * np.arange(FFT_LEN, dtype=np.int64)[None, :] % FFT_LEN) * (2.0 * np.pi / FFT_LEN)
    both = np.stack([np.cos(phase), -np.sin(phase)]) / np.sqrt(FFT_LEN)
    both = both.reshape(2, 2, 4, 32, 2, FFT_LEN).transpose(2, 4, 0, 1, 3, 5)
    return both.reshape(4, 256, FFT_LEN).astype(np.float32).astype(jnp.bfloat16)


def coordinates():
    chan, inp = lax.axis_index("chan"), lax.axis_index("inp")
    return chan % 4, chan // 4 % 4, inp // 2 * 2 + chan // 16, inp % 2


def device_at(x, y, z, core):
    return z % 2 * 16 + y * 4 + x, z // 2 * 2 + core


def away(dx, dy, dz, dcore):
    x, y, z, core = coordinates()
    return device_at((x + dx) % 4, (y + dy) % 4, (z + dz) % 8, (core + dcore) % 2)


def spectra_kernel(
    volt_hbm, window_hbm, table_hbm, out_ref,
    volt, window, table, filtered, turned, send, recv, unpacked,
    volt_sems, window_sem, table_sems, send_sem, recv_sems, met_sem,
):
    x, y, z, core = coordinates()
    me = (z % 2) * 128 + y * 32 + x * 8 + z // 2 * 2 + core
    barrier = pltpu.get_barrier_semaphore()

    def volt_copy(run):
        at = 0 if run == 0 else run * 32 + 3
        frames = pl.ds(at, 35 if run == 0 else 32)
        return pltpu.make_async_copy(volt_hbm.at[frames], volt.at[frames], volt_sems.at[run])

    window_copy = pltpu.make_async_copy(window_hbm.at[pl.ds(0, NUM_TAPS)], window, window_sem)
    table_copies = [
        pltpu.make_async_copy(table_hbm.at[(y + g) % 4], table.at[g], table_sems.at[g])
        for g in range(4)
    ]
    window_copy.start()
    for run in range(4):
        volt_copy(run).start()
    table_copies[0].start()
    for run in range(4, 8):
        volt_copy(run).start()
    for copy in table_copies[1:]:
        copy.start()

    def greet(step, carry):
        for target in (away(step % 4, step // 4, 0, 0), away(0, 0, step // 2, step % 2)):
            pl.semaphore_signal(barrier, inc=1, device_id=target, device_id_type=MESH)
        return carry

    lax.fori_loop(1, 16, greet, 0)

    def filter_run(run):
        volt_copy(run).wait()

        def block(i, carry):
            at = run * 32 + i * 16
            for q in range(4):
                rows = slice(q * 16, (q + 1) * 16)
                taps = [window[t, rows, :] for t in range(NUM_TAPS)]
                frames = []
                for s in range(16 + NUM_TAPS - 1):
                    frames.append(volt[at + s, rows, :].astype(jnp.float32))
                    if s >= NUM_TAPS - 1:
                        terms = [f * tap for f, tap in zip(frames[-NUM_TAPS:], taps)]
                        first = (s - NUM_TAPS + 1) * PITCH
                        total = (terms[0] + terms[1]) + (terms[2] + terms[3])
                        turned[q, first : first + 16, :] = total
                for r in range(16):
                    n, a = q * 4 + r // 4, r % 4
                    to = run // 4 * 512 + a * HALF + run % 4 * 32
                    to = pl.multiple_of(to + i * 16, 16)
                    column = turned[q, pl.ds(r, 16, stride=PITCH), :]
                    filtered[pl.ds(to, 16), n * 128 : (n + 1) * 128] = column.astype(jnp.bfloat16)
            return carry

        lax.fori_loop(0, 2, block, 0)

    def transform(g, half):
        parts = []
        for pair in range(2):
            at = half * 512 + pair * 256
            product = lax.dot_general(
                table[g], filtered[at : at + 256, :], (((1,), (1,)), ((), ())),
                preferred_element_type=jnp.float32,
            )
            parts += [product[:, :128].reshape(4, 64, 128), product[:, 128:].reshape(4, 64, 128)]
        block = jnp.concatenate(parts, axis=0)
        send[g, :, half] = jnp.transpose(block, (1, 0, 2)).astype(jnp.bfloat16)

    def send_group(g, half, first=0, end=64):
        def one(step, carry):
            target = away(step // 16, g, step % 8, step // 8)
            slot = target[0] // 16 * 32 + target[0] % 4 * 8 + target[1]
            source, landing = send.at[g, slot], recv.at[me]
            if half is not None:
                source, landing = source.at[half], landing.at[half]
            pltpu.make_async_remote_copy(
                src_ref=source, dst_ref=landing, send_sem=send_sem, recv_sem=recv_sems.at[g],
                device_id=target, device_id_type=MESH,
            ).start()
            return carry

        lax.fori_loop(first, end, one, 0)

    def unpack(g):
        for z_lo in range(2):
            first = z_lo * 128 + (y + 4 - g) % 4 * 32
            for half in range(2):
                got = recv[pl.ds(first, 32), half].astype(jnp.float32) * 0.0625
                unpacked[...] = got.reshape(512, 128)
                for comp in range(4):
                    part = unpacked[pl.ds(comp, 128, stride=4), :]
                    to = pl.ds(pl.multiple_of(first * 4, 128), 128)
                    lanes = comp % 2 * 256 + half * 128
                    out_ref[comp // 2, to, lanes : lanes + 128] = part.astype(jnp.bfloat16)

    def meet(step, carry):
        target = away(0, 0, step // 2, step % 2)
        pl.semaphore_signal(met_sem, inc=1, device_id=target, device_id_type=MESH)
        return carry

    window_copy.wait()
    for run in range(4):
        filter_run(run)
    pl.semaphore_wait(barrier, 30)
    lax.fori_loop(1, 16, meet, 0)
    table_copies[0].wait()
    transform(0, 0)
    send_group(0, 0, 1, 16)
    pl.semaphore_wait(met_sem, 15)
    send_group(0, 0, 16)
    table_copies[1].wait()
    transform(1, 0)
    send_group(1, 0)
    for run in range(4, 8):
        filter_run(run)
    transform(0, 1)
    send_group(0, 1, 1)
    transform(1, 1)
    send_group(1, 1)
    for g in range(2, 4):
        table_copies[g].wait()
        transform(g, 0)
        transform(g, 1)
        send_group(g, None)
    recv[pl.ds(me, 1)] = send[0, pl.ds(z % 2 * 32 + x * 8 + z // 2 * 2 + core, 1)]

    for g in range(4):
        got = recv.at[pl.ds(0, 63 if g == 0 else 64)]
        pltpu.make_async_copy(got, got, recv_sems.at[g]).wait()
        unpack(g)
    sent = recv.at[pl.ds(0, 255)]
    pltpu.make_async_copy(sent, sent, send_sem).wait()


def spectra_of(voltages, window, table):
    return pl.pallas_call(
        spectra_kernel,
        out_shape=jax.ShapeDtypeStruct((2, INPUTS, 512), jnp.bfloat16),
        in_specs=[
            pl.BlockSpec(memory_space=pltpu.HBM),
            pl.BlockSpec(memory_space=pltpu.HBM),
            pl.BlockSpec(memory_space=pltpu.HBM),
        ],
        out_specs=pl.BlockSpec(memory_space=pltpu.VMEM),
        scratch_shapes=[
            pltpu.VMEM((FRAMES, 64, 128), jnp.bfloat16),
            pltpu.VMEM((NUM_TAPS, 64, 128), jnp.float32),
            pltpu.VMEM((4, 256, FFT_LEN), jnp.bfloat16),
            pltpu.VMEM((1024, FFT_LEN), jnp.bfloat16),
            pltpu.VMEM((4, 16 * PITCH, 128), jnp.float32),
            pltpu.VMEM((4, 64, 2, 16, 128), jnp.bfloat16),
            pltpu.VMEM((DEVICES, 2, 16, 128), jnp.bfloat16),
            pltpu.VMEM((512, 128), jnp.float32),
            pltpu.SemaphoreType.DMA((8,)),
            pltpu.SemaphoreType.DMA,
            pltpu.SemaphoreType.DMA((4,)),
            pltpu.SemaphoreType.DMA,
            pltpu.SemaphoreType.DMA((4,)),
            pltpu.SemaphoreType.REGULAR,
        ],
        compiler_params=pltpu.CompilerParams(
            collective_id=0, has_side_effects=True, vmem_limit_bytes=50 << 20
        ),
        name="spectra_exchange",
    )(voltages, window, table)


def gram_kernel(in_ref, out_hbm, blocks, sems):
    dims = (((1,), (1,)), ((), ()))
    down = lax.broadcasted_iota(jnp.int32, (256, 256), 0)
    across = lax.broadcasted_iota(jnp.int32, (256, 256), 1)
    copies = []
    for c in range(2):
        for k in range(4):
            rows = slice(k * 256, (k + 1) * 256)
            real = lax.dot_general(
                in_ref[c, rows, :], in_ref[c, k * 256 :, :], dims,
                preferred_element_type=jnp.float32,
            )
            turned = jnp.concatenate([in_ref[c, rows, 256:], -in_ref[c, rows, :256]], axis=1)
            imag = lax.dot_general(
                turned, in_ref[c, : (k + 1) * 256, :], dims, preferred_element_type=jnp.float32
            )
            if k > 0:
                blocks[c, rows, : k * 256] = imag[:, : k * 256]
            blocks[c, rows, rows] = jnp.where(down <= across, real[:, :256], imag[:, k * 256 :])
            if k < 3:
                blocks[c, rows, (k + 1) * 256 :] = real[:, 256:]
            copy = pltpu.make_async_copy(blocks.at[c, rows], out_hbm.at[c, rows], sems.at[c * 4 + k])
            copy.start()
            copies.append(copy)
    for copy in copies:
        copy.wait()


def gram(spectra):
    return pl.pallas_call(
        gram_kernel,
        out_shape=jax.ShapeDtypeStruct((2, INPUTS, INPUTS), jnp.float32),
        in_specs=[pl.BlockSpec(memory_space=pltpu.VMEM)],
        out_specs=pl.BlockSpec(memory_space=pltpu.HBM),
        scratch_shapes=[
            pltpu.VMEM((2, INPUTS, INPUTS), jnp.float32),
            pltpu.SemaphoreType.DMA((8,)),
        ],
        compiler_params=pltpu.CompilerParams(vmem_limit_bytes=40 << 20),
        name="gram",
    )(spectra)


def local(voltages):
    tiles = voltages.reshape(4, FRAMES * 16, 128).transpose(1, 0, 2).reshape(FRAMES, 64, 128)
    return gram(spectra_of(tiles, jnp.asarray(make_window()), jnp.asarray(make_table())))


def solution(mesh):
    in_specs = (P(("chan", "inp"), None),)
    out_specs = P(("chan", "inp"), None, None)
    return jax.shard_map(local, mesh=mesh, in_specs=in_specs, out_specs=out_specs, check_vma=False)
```

time: 75.1 us -> 65.9 us (0.88)
  local copies, waits for them, and re-layouts: 5.29 us -> 0 us
  Pallas kernels: 69.6 us -> 65.8 us
    unnamed x6 -> x0, local copies, waits for them, and re-layouts: 5.29 us -> none
    pallas_call x1, Pallas kernels: 6.7 us -> 4.01 us  [gram(): pl.pallas_call(gram_kernel, out_shape=jax.ShapeDtypeStruct((2, INPUTS, IN...]
    pallas_call x1, Pallas kernels: 62.9 us -> 61.8 us  [spectra_of(): pl.pallas_call(spectra_kernel, out_shape=jax.ShapeDtypeStruct((2, INPUTS,...]
where the time goes in v3:
time: 65.9 us; the launch traced here: 65.8 us
  Pallas kernels  65.8 us (100%)
    pallas_call x1, Pallas kernels, spectra_of(): pl.pallas_call(spectra_kernel, out_shape=jax.ShapeDtypeStruct((2, INPUTS,...  61.8 us
    pallas_call x1, Pallas kernels, gram(): pl.pallas_call(gram_kernel, out_shape=jax.ShapeDtypeStruct((2, INPUTS, IN...  4.01 us

profile of v3, /device:TPU:1, one launch (start us, length us, event | category | flops | bytes accessed | tf_op | source)
XLA Modules:
  0.0 65.8 jit_solution(12559619950178931979)
XLA Ops:
  0.0 61.8 %spectra_exchange.1.in_ref = bf16[2,1024,512]{2,1,0:T(8,128)(2,1)S(1)} custom-call(bf16[259,64,128]{2,1,0:T(8,128)(2,1)} %bitcast.5, f32[96,64,128]{2,1,0:T(8,128)} %constant.4.clone.window_hbm, bf16[4,256,2048]{2,1,0:T(8,128)(2,1)} %constant.5.clone.table_hbm), custom_call_target="tpu_custom_call" | custom-call | tf_op jit(solution)/shard_map/spectra_exchange/pallas_call | solution.py:193
  61.8 4.0 %gram.1 = f32[2,1024,1024]{2,1,0:T(8,128)} custom-call(bf16[2,1024,512]{2,1,0:T(8,128)(2,1)S(1)} %spectra_exchange.1.in_ref), custom_call_target="tpu_custom_call" | custom-call | tf_op jit(solution)/shard_map/gram/pallas_call | solution.py:254

commit v4 on v3

--- a/solution.py
+++ b/solution.py
@@ -36,18 +36,23 @@
     return both.reshape(4, 256, FFT_LEN).astype(np.float32).astype(jnp.bfloat16)
 
 
-def coordinates():
-    chan, inp = lax.axis_index("chan"), lax.axis_index("inp")
-    return chan % 4, chan // 4 % 4, inp // 2 * 2 + chan // 16, inp % 2
-
-
-def device_at(x, y, z, core):
-    return z % 2 * 16 + y * 4 + x, z // 2 * 2 + core
-
-
-def away(dx, dy, dz, dcore):
-    x, y, z, core = coordinates()
-    return device_at((x + dx) % 4, (y + dy) % 4, (z + dz) % 8, (core + dcore) % 2)
+class Torus:
+    def __init__(self):
+        chan, inp = lax.axis_index("chan"), lax.axis_index("inp")
+        self.x, self.y = lax.rem(chan, 4), lax.rem(lax.div(chan, 4), 4)
+        self.z, self.core = lax.div(inp, 2) * 2 + lax.div(chan, 16), lax.rem(inp, 2)
+        self.flat = chan * 8 + inp
+        self.slot = lax.div(chan, 16) * 32 + self.x * 8 + inp
+        zs = [lax.rem(self.z + dz, 8) for dz in range(8)]
+        self.z_chan = [lax.rem(z, 2) * 16 for z in zs]
+        self.z_inp = [lax.div(z, 2) * 2 for z in zs]
+        self.lead = [jnp.where(z == 0, 3, jnp.where(z < 3, 2, jnp.where(z == 3, 1, 0))) for z in zs]
+        self.y_chan = [lax.rem(self.y + dy, 4) * 4 for dy in range(4)]
+
+    def away(self, dx, dy, dz, dcore):
+        x, core = lax.rem(self.x + dx, 4), lax.rem(self.core + dcore, 2)
+        inp = self.z_inp[dz] + core
+        return (self.z_chan[dz] + self.y_chan[dy] + x, inp), self.z_chan[dz] * 2 + x * 8 + inp
 
 
 def spectra_kernel(
@@ -55,8 +60,9 @@
     volt, window, table, filtered, turned, send, recv, unpacked,
     volt_sems, window_sem, table_sems, send_sem, recv_sems, met_sem,
 ):
-    x, y, z, core = coordinates()
-    me = (z % 2) * 128 + y * 32 + x * 8 + z // 2 * 2 + core
+    here = Torus()
+    me, y = here.flat, here.y
+    across = [here.away(0, dy, 0, 0)[0] for dy in range(1, 4)]
     barrier = pltpu.get_barrier_semaphore()
 
     def volt_copy(run):
@@ -66,24 +72,33 @@
 
     window_copy = pltpu.make_async_copy(window_hbm.at[pl.ds(0, NUM_TAPS)], window, window_sem)
     table_copies = [
-        pltpu.make_async_copy(table_hbm.at[(y + g) % 4], table.at[g], table_sems.at[g])
+        pltpu.make_async_copy(table_hbm.at[lax.rem(y + g, 4)], table.at[g], table_sems.at[g])
         for g in range(4)
     ]
     window_copy.start()
-    for run in range(4):
-        volt_copy(run).start()
+    volt_copy(0).start()
+    volt_copy(1).start()
+
+    def greet(dx, dcore, first=0):
+        for dz in range(first, 8):
+            target = here.away(dx, 0, dz, dcore)[0]
+            pl.semaphore_signal(barrier, inc=1, device_id=target, device_id_type=MESH)
+
+    def greet_eight(k, carry):
+        greet(lax.div(k, 2), lax.rem(k, 2))
+        return carry
+
+    greet(0, 0, 1)
+    lax.fori_loop(1, 8, greet_eight, 0)
+    for target in across:
+        pl.semaphore_signal(barrier, inc=1, device_id=target, device_id_type=MESH)
+    volt_copy(2).start()
+    volt_copy(3).start()
     table_copies[0].start()
     for run in range(4, 8):
         volt_copy(run).start()
     for copy in table_copies[1:]:
         copy.start()
-
-    def greet(step, carry):
-        for target in (away(step % 4, step // 4, 0, 0), away(0, 0, step // 2, step % 2)):
-            pl.semaphore_signal(barrier, inc=1, device_id=target, device_id_type=MESH)
-        return carry
-
-    lax.fori_loop(1, 16, greet, 0)
 
     def filter_run(run):
         volt_copy(run).wait()
@@ -123,10 +138,9 @@
         block = jnp.concatenate(parts, axis=0)
         send[g, :, half] = jnp.transpose(block, (1, 0, 2)).astype(jnp.bfloat16)
 
-    def send_group(g, half, first=0, end=64):
-        def one(step, carry):
-            target = away(step // 16, g, step % 8, step // 8)
-            slot = target[0] // 16 * 32 + target[0] % 4 * 8 + target[1]
+    def send_eight(g, half, dx, dcore, first=0):
+        for dz in range(first, 8):
+            target, slot = here.away(dx, g, dz, dcore)
             source, landing = send.at[g, slot], recv.at[me]
             if half is not None:
                 source, landing = source.at[half], landing.at[half]
@@ -134,13 +148,17 @@
                 src_ref=source, dst_ref=landing, send_sem=send_sem, recv_sem=recv_sems.at[g],
                 device_id=target, device_id_type=MESH,
             ).start()
+
+    def send_group(g, half, first=0):
+        def eight(k, carry):
+            send_eight(g, half, lax.div(k, 2), lax.rem(k, 2))
             return carry
 
-        lax.fori_loop(first, end, one, 0)
+        lax.fori_loop(first, 8, eight, 0)
 
     def unpack(g):
         for z_lo in range(2):
-            first = z_lo * 128 + (y + 4 - g) % 4 * 32
+            first = z_lo * 128 + lax.rem(y + 4 - g, 4) * 32
             for half in range(2):
                 got = recv[pl.ds(first, 32), half].astype(jnp.float32) * 0.0625
                 unpacked[...] = got.reshape(512, 128)
@@ -150,27 +168,24 @@
                     lanes = comp % 2 * 256 + half * 128
                     out_ref[comp // 2, to, lanes : lanes + 128] = part.astype(jnp.bfloat16)
 
-    def meet(step, carry):
-        target = away(0, 0, step // 2, step % 2)
-        pl.semaphore_signal(met_sem, inc=1, device_id=target, device_id_type=MESH)
-        return carry
-
     window_copy.wait()
     for run in range(4):
         filter_run(run)
-    pl.semaphore_wait(barrier, 30)
-    lax.fori_loop(1, 16, meet, 0)
+    pl.semaphore_wait(barrier, 66)
+    for target in across:
+        pl.semaphore_signal(met_sem, inc=1, device_id=target, device_id_type=MESH)
     table_copies[0].wait()
     transform(0, 0)
-    send_group(0, 0, 1, 16)
-    pl.semaphore_wait(met_sem, 15)
-    send_group(0, 0, 16)
+    send_eight(0, 0, 0, 0, 1)
+    send_group(0, 0, 1)
+    pl.semaphore_wait(met_sem, 3)
     table_copies[1].wait()
     transform(1, 0)
     send_group(1, 0)
     for run in range(4, 8):
         filter_run(run)
     transform(0, 1)
+    send_eight(0, 1, 0, 0, 1)
     send_group(0, 1, 1)
     transform(1, 1)
     send_group(1, 1)
@@ -178,8 +193,34 @@
         table_copies[g].wait()
         transform(g, 0)
         transform(g, 1)
-        send_group(g, None)
-    recv[pl.ds(me, 1)] = send[0, pl.ds(z % 2 * 32 + x * 8 + z // 2 * 2 + core, 1)]
+
+    def send_one(j, dz):
+        g, k = lax.div(j, 8), lax.rem(j, 8)
+        x, core = lax.rem(here.x + lax.div(k, 2), 4), lax.rem(here.core + lax.rem(k, 2), 2)
+        inp = here.z_inp[dz] + core
+        target = (here.z_chan[dz] + lax.rem(here.y + 2 + g, 4) * 4 + x, inp)
+        pltpu.make_async_remote_copy(
+            src_ref=send.at[2 + g, here.z_chan[dz] * 2 + x * 8 + inp], dst_ref=recv.at[me],
+            send_sem=send_sem, recv_sem=recv_sems.at[2 + g],
+            device_id=target, device_id_type=MESH,
+        ).start()
+
+    def rounds(j, carry):
+        for dz in range(8):
+            lead = here.lead[dz]
+
+            @pl.when(j < 16 - lead)
+            def _():
+                send_one(j, dz)
+
+            @pl.when((lax.rem(j, 4) == 3) & (lax.div(j, 4) < lead))
+            def _():
+                send_one(16 - lead + lax.div(j, 4), dz)
+
+        return carry
+
+    lax.fori_loop(0, 16, rounds, 0)
+    recv[pl.ds(me, 1)] = send[0, pl.ds(here.slot, 1)]
 
     for g in range(4):
         got = recv.at[pl.ds(0, 63 if g == 0 else 64)]

time: 65.9 us -> 63.3 us (0.961)
  the two profiles are of different devices: /device:TPU:1 before, /device:TPU:33 now
where the time goes in v4:
time: 63.3 us; the launch traced here: 63.2 us
  Pallas kernels  63.2 us (100%)
    pallas_call x1, Pallas kernels, spectra_of(): pl.pallas_call(spectra_kernel, out_shape=jax.ShapeDtypeStruct((2, INPUTS,...  59.1 us
    pallas_call x1, Pallas kernels, gram(): pl.pallas_call(gram_kernel, out_shape=jax.ShapeDtypeStruct((2, INPUTS, IN...  4.02 us

profile of v4, /device:TPU:33, one launch (start us, length us, event | category | flops | bytes accessed | tf_op | source)
XLA Modules:
  0.0 63.2 jit_solution(16509275600456450214)
XLA Ops:
  0.0 59.1 %spectra_exchange.1.in_ref = bf16[2,1024,512]{2,1,0:T(8,128)(2,1)S(1)} custom-call(bf16[259,64,128]{2,1,0:T(8,128)(2,1)} %bitcast.5, f32[96,64,128]{2,1,0:T(8,128)} %constant.4.clone.window_hbm, bf16[4,256,2048]{2,1,0:T(8,128)(2,1)} %constant.5.clone.table_hbm), custom_call_target="tpu_custom_call" | custom-call | tf_op jit(solution)/shard_map/spectra_exchange/pallas_call | solution.py:234
  59.2 4.0 %gram.1 = f32[2,1024,1024]{2,1,0:T(8,128)} custom-call(bf16[2,1024,512]{2,1,0:T(8,128)(2,1)S(1)} %spectra_exchange.1.in_ref), custom_call_target="tpu_custom_call" | custom-call | tf_op jit(solution)/shard_map/gram/pallas_call | solution.py:295

commit v5 on v4

v5 whole, which is shorter than its diff:
```python
import jax
import jax.numpy as jnp
import numpy as np
from jax import lax
from jax.experimental import pallas as pl
from jax.experimental.pallas import tpu as pltpu
from jax.sharding import PartitionSpec as P

FFT_LEN = 2048
CHANNELS = 512
NUM_TAPS = 4
SPECTRA = 256
FRAMES = SPECTRA + NUM_TAPS - 1
INPUTS = 1024
DEVICES = 256
HALF = SPECTRA // 2
PITCH = 17
WINDOW_PAD = 192
MESH = pl.DeviceIdType.MESH


def make_window():
    index = np.arange(NUM_TAPS * FFT_LEN, dtype=np.float64) + 0.5
    shifted = index / FFT_LEN - NUM_TAPS / 2.0
    taper = 0.54 - 0.46 * np.cos(2.0 * np.pi * index / (NUM_TAPS * FFT_LEN))
    window = (np.sinc(shifted) * taper).astype(np.float32).reshape(NUM_TAPS, 16, 1, 128)
    window = np.broadcast_to(window, (NUM_TAPS, 16, 4, 128)).reshape(NUM_TAPS, 64, 128)
    return np.concatenate([window, np.zeros((WINDOW_PAD - NUM_TAPS, 64, 128), np.float32)])


def make_table():
    bins = np.arange(CHANNELS, dtype=np.int64)[:, None] + FFT_LEN // 8
    phase = (bins * np.arange(FFT_LEN, dtype=np.int64)[None, :] % FFT_LEN) * (2.0 * np.pi / FFT_LEN)
    both = np.stack([np.cos(phase), -np.sin(phase)]) / np.sqrt(FFT_LEN)
    both = both.reshape(2, 2, 4, 32, 2, FFT_LEN).transpose(2, 4, 0, 1, 3, 5)
    return both.reshape(4, 256, FFT_LEN).astype(np.float32).astype(jnp.bfloat16)


class Torus:
    def __init__(self):
        chan, inp = lax.axis_index("chan"), lax.axis_index("inp")
        self.x, self.y = lax.rem(chan, 4), lax.rem(lax.div(chan, 4), 4)
        self.z, self.core = lax.div(inp, 2) * 2 + lax.div(chan, 16), lax.rem(inp, 2)
        self.flat = chan * 8 + inp
        self.slot = lax.div(chan, 16) * 32 + self.x * 8 + inp
        zs = [lax.rem(self.z + dz, 8) for dz in range(8)]
        self.z_chan = [lax.rem(z, 2) * 16 for z in zs]
        self.z_inp = [lax.div(z, 2) * 2 for z in zs]
        self.lead = [jnp.where(z == 0, 6, jnp.where(z < 3, 4, jnp.where(z == 3, 2, 0))) for z in zs]
        self.y_chan = [lax.rem(self.y + dy, 4) * 4 for dy in range(4)]

    def away(self, dx, dy, dz, dcore):
        x, core = lax.rem(self.x + dx, 4), lax.rem(self.core + dcore, 2)
        inp = self.z_inp[dz] + core
        return (self.z_chan[dz] + self.y_chan[dy] + x, inp), self.z_chan[dz] * 2 + x * 8 + inp

    def across(self, dx, dy):
        x = self.x + (1 - 2 * lax.rem(self.x, 2)) * dx
        return self.z_chan[0] + self.y_chan[dy] + x, self.z_inp[0] + self.core


def gram_rows(in_ref, out_ref, k):
    dims = (((1,), (1,)), ((), ()))
    rows = slice(k * 256, (k + 1) * 256)
    real = lax.dot_general(
        in_ref[rows, :], in_ref[k * 256 :, :], dims, preferred_element_type=jnp.float32
    )
    turned = jnp.concatenate([in_ref[rows, 256:], -in_ref[rows, :256]], axis=1)
    imag = lax.dot_general(
        turned, in_ref[: (k + 1) * 256, :], dims, preferred_element_type=jnp.float32
    )
    down = lax.broadcasted_iota(jnp.int32, (256, 256), 0)
    across = lax.broadcasted_iota(jnp.int32, (256, 256), 1)
    if k > 0:
        out_ref[rows, : k * 256] = imag[:, : k * 256]
    out_ref[rows, rows] = jnp.where(down <= across, real[:, :256], imag[:, k * 256 :])
    if k < 3:
        out_ref[rows, (k + 1) * 256 :] = real[:, 256:]


def spectra_kernel(
    volt_hbm, window_hbm, table_hbm, first_ref, second_ref,
    volt, window, table, filtered, turned, send, recv, unpacked, channel,
    volt_sems, window_sem, table_sems, send_sem, recv_sems, met_sem,
):
    here = Torus()
    me, y = here.flat, here.y
    across = [here.across(dx, dy) for dx in range(2) for dy in range(4) if dx + dy > 0]
    barrier = pltpu.get_barrier_semaphore()

    def volt_copy(run):
        at = 0 if run == 0 else run * 32 + 3
        frames = pl.ds(at, 35 if run == 0 else 32)
        return pltpu.make_async_copy(volt_hbm.at[frames], volt.at[frames], volt_sems.at[run])

    window_copy = pltpu.make_async_copy(window_hbm.at[pl.ds(0, NUM_TAPS)], window, window_sem)
    table_copies = [
        pltpu.make_async_copy(table_hbm.at[lax.rem(y + g, 4)], table.at[g], table_sems.at[g])
        for g in range(4)
    ]
    window_copy.start()
    volt_copy(0).start()
    volt_copy(1).start()

    def greet(dx, dcore, first=0):
        for dz in range(first, 8):
            target = here.away(dx, 0, dz, dcore)[0]
            pl.semaphore_signal(barrier, inc=1, device_id=target, device_id_type=MESH)

    greet(0, 0, 1)
    greet(0, 1)
    greet(2, 0)
    greet(2, 1)
    for target in across:
        pl.semaphore_signal(barrier, inc=1, device_id=target, device_id_type=MESH)
    volt_copy(2).start()
    volt_copy(3).start()
    table_copies[0].start()
    for run in range(4, 8):
        volt_copy(run).start()
    for copy in table_copies[1:]:
        copy.start()

    def filter_run(run):
        volt_copy(run).wait()

        def block(i, carry):
            at = run * 32 + i * 16
            for q in range(4):
                rows = slice(q * 16, (q + 1) * 16)
                taps = [window[t, rows, :] for t in range(NUM_TAPS)]
                frames = []
                for s in range(16 + NUM_TAPS - 1):
                    frames.append(volt[at + s, rows, :].astype(jnp.float32))
                    if s >= NUM_TAPS - 1:
                        terms = [f * tap for f, tap in zip(frames[-NUM_TAPS:], taps)]
                        first = (s - NUM_TAPS + 1) * PITCH
                        total = (terms[0] + terms[1]) + (terms[2] + terms[3])
                        turned[q, first : first + 16, :] = total
                for r in range(16):
                    n, a = q * 4 + r // 4, r % 4
                    to = run // 4 * 512 + a * HALF + run % 4 * 32
                    to = pl.multiple_of(to + i * 16, 16)
                    column = turned[q, pl.ds(r, 16, stride=PITCH), :]
                    filtered[pl.ds(to, 16), n * 128 : (n + 1) * 128] = column.astype(jnp.bfloat16)
            return carry

        lax.fori_loop(0, 2, block, 0)

    def products(g, half):
        parts = []
        for pair in range(2):
            at = half * 512 + pair * 256
            product = lax.dot_general(
                table[g], filtered[at : at + 256, :], (((1,), (1,)), ((), ())),
                preferred_element_type=jnp.float32,
            )
            parts += [product[:, :128].reshape(4, 64, 128), product[:, 128:].reshape(4, 64, 128)]
        return parts

    def transform(g, half):
        block = jnp.concatenate(products(g, half), axis=0)
        send[g, :, half] = jnp.transpose(block, (1, 0, 2)).astype(jnp.bfloat16)

    def transform_channels(g):
        halves = [products(g, 0), products(g, 1)]
        for c in range(2):
            rows = [halves[h][a][c * 2 : c * 2 + 2] for a in range(4) for h in range(2)]
            block = jnp.concatenate(rows, axis=0)
            send[g, :, c] = jnp.transpose(block, (1, 0, 2)).astype(jnp.bfloat16)

    def send_eight(g, tile, dx, dcore, first=0):
        for dz in range(first, 8):
            target, slot = here.away(dx, g, dz, dcore)
            pltpu.make_async_remote_copy(
                src_ref=send.at[g, slot, tile], dst_ref=recv.at[me, tile],
                send_sem=send_sem, recv_sem=recv_sems.at[g, tile],
                device_id=target, device_id_type=MESH,
            ).start()

    def send_group(g, tile, first=0):
        def eight(k, carry):
            send_eight(g, tile, lax.div(k, 2), lax.rem(k, 2))
            return carry

        lax.fori_loop(first, 8, eight, 0)

    def unpack(g, tile):
        got = recv.at[pl.ds(0, 63 if g == 0 else 64), 0]
        pltpu.make_async_copy(got, got, recv_sems.at[g, tile]).wait()
        for z_lo in range(2):
            first = z_lo * 128 + lax.rem(y + 4 - g, 4) * 32
            values = recv[pl.ds(first, 32), tile].astype(jnp.float32) * 0.0625
            unpacked[...] = values.reshape(512, 128)
            to = pl.ds(pl.multiple_of(first * 4, 128), 128)
            for k in range(4):
                part = unpacked[pl.ds(k, 128, stride=4), :].astype(jnp.bfloat16)
                c, half = (k // 2, tile) if g < 2 else (tile, k // 2)
                lanes = k % 2 * 256 + half * 128
                (channel, second_ref)[c][to, lanes : lanes + 128] = part

    window_copy.wait()
    for run in range(4):
        filter_run(run)
    pl.semaphore_wait(barrier, 38)
    for target in across:
        pl.semaphore_signal(met_sem, inc=1, device_id=target, device_id_type=MESH)
    table_copies[0].wait()
    transform(0, 0)
    send_eight(0, 0, 0, 0, 1)
    send_eight(0, 0, 0, 1)
    send_eight(0, 0, 2, 0)
    send_eight(0, 0, 2, 1)
    pl.semaphore_wait(met_sem, 7)
    for dx in (1, 3):
        send_eight(0, 0, dx, 0)
        send_eight(0, 0, dx, 1)
    table_copies[1].wait()
    transform(1, 0)
    send_group(1, 0)
    for run in range(4, 8):
        filter_run(run)
    transform(0, 1)
    send_eight(0, 1, 0, 0, 1)
    send_group(0, 1, 1)
    transform(1, 1)
    send_group(1, 1)
    for g in range(2, 4):
        table_copies[g].wait()
        transform_channels(g)

    def send_one(j, dz):
        tile, g, k = lax.div(j, 16), lax.rem(lax.div(j, 8), 2), lax.rem(j, 8)
        x, core = lax.rem(here.x + lax.div(k, 2), 4), lax.rem(here.core + lax.rem(k, 2), 2)
        inp = here.z_inp[dz] + core
        target = (here.z_chan[dz] + lax.rem(here.y + 2 + g, 4) * 4 + x, inp)
        pltpu.make_async_remote_copy(
            src_ref=send.at[2 + g, here.z_chan[dz] * 2 + x * 8 + inp, tile], dst_ref=recv.at[me, tile],
            send_sem=send_sem, recv_sem=recv_sems.at[2 + g, tile],
            device_id=target, device_id_type=MESH,
        ).start()

    def to_origin(j, dz):
        k = lax.rem(j, 8)
        apart = lax.rem(here.x + lax.div(k, 2), 4) + lax.rem(here.y + 2 + lax.rem(lax.div(j, 8), 2), 4)
        core = lax.rem(here.core + lax.rem(k, 2), 2)
        return apart + here.z_chan[dz] + here.z_inp[dz] + 1 - core == 0

    def rounds(j, carry):
        for dz in range(8):
            lead = jnp.where(to_origin(j, dz), 16, here.lead[dz])

            @pl.when(j < 32 - lead)
            def _():
                send_one(j, dz)

            ahead = 32 - here.lead[dz] + lax.div(j, 4)

            @pl.when((lax.rem(j, 4) == 3) & (ahead < 32))
            def _():
                @pl.when(jnp.logical_not(to_origin(ahead, dz)))
                def _():
                    send_one(ahead, dz)

            @pl.when((j < 16) & to_origin(j, dz))
            def _():
                send_one(j + 16, dz)

        return carry

    lax.fori_loop(0, 32, rounds, 0)
    recv[pl.ds(me, 1)] = send[0, pl.ds(here.slot, 1)]

    for g, tile in ((0, 0), (1, 0), (0, 1), (1, 1), (2, 0), (3, 0)):
        unpack(g, tile)
    for k in range(4):
        gram_rows(channel, first_ref, k)
    unpack(2, 1)
    unpack(3, 1)
    sent = recv.at[pl.ds(0, 255)]
    pltpu.make_async_copy(sent, sent, send_sem).wait()


def spectra_of(voltages, window, table):
    return pl.pallas_call(
        spectra_kernel,
        out_shape=(
            jax.ShapeDtypeStruct((INPUTS, INPUTS), jnp.float32),
            jax.ShapeDtypeStruct((INPUTS, 512), jnp.bfloat16),
        ),
        in_specs=[
            pl.BlockSpec(memory_space=pltpu.HBM),
            pl.BlockSpec(memory_space=pltpu.HBM),
            pl.BlockSpec(memory_space=pltpu.HBM),
        ],
        out_specs=(pl.BlockSpec(memory_space=pltpu.VMEM),) * 2,
        scratch_shapes=[
            pltpu.VMEM((FRAMES, 64, 128), jnp.bfloat16),
            pltpu.VMEM((NUM_TAPS, 64, 128), jnp.float32),
            pltpu.VMEM((4, 256, FFT_LEN), jnp.bfloat16),
            pltpu.VMEM((1024, FFT_LEN), jnp.bfloat16),
            pltpu.VMEM((4, 16 * PITCH, 128), jnp.float32),
            pltpu.VMEM((4, 64, 2, 16, 128), jnp.bfloat16),
            pltpu.VMEM((DEVICES, 2, 16, 128), jnp.bfloat16),
            pltpu.VMEM((512, 128), jnp.float32),
            pltpu.VMEM((INPUTS, 512), jnp.bfloat16),
            pltpu.SemaphoreType.DMA((8,)),
            pltpu.SemaphoreType.DMA,
            pltpu.SemaphoreType.DMA((4,)),
            pltpu.SemaphoreType.DMA,
            pltpu.SemaphoreType.DMA((4, 2)),
            pltpu.SemaphoreType.REGULAR,
        ],
        compiler_params=pltpu.CompilerParams(
            collective_id=0, has_side_effects=True, vmem_limit_bytes=45 << 20
        ),
        name="spectra_exchange",
    )(voltages, window, table)


def gram_kernel(first_ref, in_ref, out_hbm, blocks, first_sems, sems):
    copies = []
    for k in range(2):
        rows = slice(k * 512, (k + 1) * 512)
        copies.append(pltpu.make_async_copy(first_ref.at[rows], out_hbm.at[0, rows], first_sems.at[k]))
        copies[-1].start()
    for k in range(4):
        rows = slice(k * 256, (k + 1) * 256)
        gram_rows(in_ref, blocks, k)
        copies.append(pltpu.make_async_copy(blocks.at[rows], out_hbm.at[1, rows], sems.at[k]))
        copies[-1].start()
    for copy in copies:
        copy.wait()


def gram(first, spectra):
    return pl.pallas_call(
        gram_kernel,
        out_shape=jax.ShapeDtypeStruct((2, INPUTS, INPUTS), jnp.float32),
        in_specs=[pl.BlockSpec(memory_space=pltpu.VMEM)] * 2,
        out_specs=pl.BlockSpec(memory_space=pltpu.HBM),
        scratch_shapes=[
            pltpu.VMEM((INPUTS, INPUTS), jnp.float32),
            pltpu.SemaphoreType.DMA((2,)),
            pltpu.SemaphoreType.DMA((4,)),
        ],
        compiler_params=pltpu.CompilerParams(vmem_limit_bytes=40 << 20),
        name="gram",
    )(first, spectra)


def local(voltages):
    tiles = voltages.reshape(4, FRAMES * 16, 128).transpose(1, 0, 2).reshape(FRAMES, 64, 128)
    return gram(*spectra_of(tiles, jnp.asarray(make_window()), jnp.asarray(make_table())))


def solution(mesh):
    in_specs = (P(("chan", "inp"), None),)
    out_specs = P(("chan", "inp"), None, None)
    return jax.shard_map(local, mesh=mesh, in_specs=in_specs, out_specs=out_specs, check_vma=False)
```

time: 63.3 us -> 62.3 us (0.984)
  Pallas kernels: 63.2 us -> 62.2 us
    pallas_call x1, Pallas kernels: 4.02 us -> 3.35 us  [gram(): pl.pallas_call(gram_kernel, out_shape=jax.ShapeDtypeStruct((2, INPUTS, IN...]
where the time goes in v5:
time: 62.3 us
  Pallas kernels  62.2 us (100%)
    pallas_call x1, Pallas kernels, spectra_of(): pl.pallas_call(spectra_kernel, out_shape=(jax.ShapeDtypeStruct((INPUTS, I...  58.9 us
    pallas_call x1, Pallas kernels, gram(): pl.pallas_call(gram_kernel, out_shape=jax.ShapeDtypeStruct((2, INPUTS, IN...  3.35 us

profile of v5, /device:TPU:33, one launch (start us, length us, event | category | flops | bytes accessed | tf_op | source)
XLA Modules:
  0.0 62.3 jit_solution(3627500081202072173)
XLA Ops:
  0.0 58.9 %spectra_exchange.1 = (f32[1024,1024]{1,0:T(8,128)S(1)}, bf16[1024,512]{1,0:T(8,128)(2,1)S(1)}) custom-call(bf16[259,64,128]{2,1,0:T(8,128)(2,1)} %bitcast.5, f32[192,64,128]{2,1,0:T(8,128)} %constant.4.clone.window_hbm, bf16[4,256,2048]{2,1,0:T(8,128)(2,1)} %constant.5.clone.table_hbm), custom_call_target="tpu_custom_call" | custom-call | tf_op jit(solution)/shard_map/spectra_exchange/pallas_call | solution.py:285
  58.9 3.4 %gram.1 = f32[2,1024,1024]{2,1,0:T(8,128)} custom-call(f32[1024,1024]{1,0:T(8,128)S(1)} %get-tuple-element.7.first_ref, bf16[1024,512]{1,0:T(8,128)(2,1)S(1)} %get-tuple-element.8.in_ref), custom_call_target="tpu_custom_call" | custom-call | tf_op jit(solution)/shard_map/gram/pallas_call | solution.py:337

commit v6 on v5

--- a/solution.py
+++ b/solution.py
@@ -191,7 +191,7 @@
         for z_lo in range(2):
             first = z_lo * 128 + lax.rem(y + 4 - g, 4) * 32
             values = recv[pl.ds(first, 32), tile].astype(jnp.float32) * 0.0625
-            unpacked[...] = values.reshape(512, 128)
+            unpacked[:512, :] = values.reshape(512, 128)
             to = pl.ds(pl.multiple_of(first * 4, 128), 128)
             for k in range(4):
                 part = unpacked[pl.ds(k, 128, stride=4), :].astype(jnp.bfloat16)
@@ -299,10 +299,10 @@
             pltpu.VMEM((NUM_TAPS, 64, 128), jnp.float32),
             pltpu.VMEM((4, 256, FFT_LEN), jnp.bfloat16),
             pltpu.VMEM((1024, FFT_LEN), jnp.bfloat16),
-            pltpu.VMEM((4, 16 * PITCH, 128), jnp.float32),
+            pltpu.VMEM((4, 17 * PITCH + 7, 128), jnp.float32),
             pltpu.VMEM((4, 64, 2, 16, 128), jnp.bfloat16),
             pltpu.VMEM((DEVICES, 2, 16, 128), jnp.bfloat16),
-            pltpu.VMEM((512, 128), jnp.float32),
+            pltpu.VMEM((520, 128), jnp.float32),
             pltpu.VMEM((INPUTS, 512), jnp.bfloat16),
             pltpu.SemaphoreType.DMA((8,)),
             pltpu.SemaphoreType.DMA,

time: 62.3 us -> 62.3 us (level)
  no operation moved by 1% of the time
where the time goes in v6:
time: 62.3 us
  Pallas kernels  62.2 us (100%)
    pallas_call x1, Pallas kernels, spectra_of(): pl.pallas_call(spectra_kernel, out_shape=(jax.ShapeDtypeStruct((INPUTS, I...  58.9 us
    pallas_call x1, Pallas kernels, gram(): pl.pallas_call(gram_kernel, out_shape=jax.ShapeDtypeStruct((2, INPUTS, IN...  3.35 us

profile of v6, /device:TPU:33, one launch (start us, length us, event | category | flops | bytes accessed | tf_op | source)
XLA Modules:
  0.0 62.3 jit_solution(17610412997671142495)
XLA Ops:
  0.0 58.9 %spectra_exchange.1 = (f32[1024,1024]{1,0:T(8,128)S(1)}, bf16[1024,512]{1,0:T(8,128)(2,1)S(1)}) custom-call(bf16[259,64,128]{2,1,0:T(8,128)(2,1)} %bitcast.5, f32[192,64,128]{2,1,0:T(8,128)} %constant.4.clone.window_hbm, bf16[4,256,2048]{2,1,0:T(8,128)(2,1)} %constant.5.clone.table_hbm), custom_call_target="tpu_custom_call" | custom-call | tf_op jit(solution)/shard_map/spectra_exchange/pallas_call | solution.py:285
  58.9 3.4 %gram.1 = f32[2,1024,1024]{2,1,0:T(8,128)} custom-call(f32[1024,1024]{1,0:T(8,128)S(1)} %get-tuple-element.7.first_ref, bf16[1024,512]{1,0:T(8,128)(2,1)S(1)} %get-tuple-element.8.in_ref), custom_call_target="tpu_custom_call" | custom-call | tf_op jit(solution)/shard_map/gram/pallas_call | solution.py:337

commit v7 on v6

--- a/solution.py
+++ b/solution.py
@@ -46,7 +46,7 @@
         zs = [lax.rem(self.z + dz, 8) for dz in range(8)]
         self.z_chan = [lax.rem(z, 2) * 16 for z in zs]
         self.z_inp = [lax.div(z, 2) * 2 for z in zs]
-        self.lead = [jnp.where(z == 0, 6, jnp.where(z < 3, 4, jnp.where(z == 3, 2, 0))) for z in zs]
+        self.lead = [jnp.where(z < 2, 6 - z, jnp.where(z == 2, 4, jnp.where(z == 3, 2, 0))) for z in zs]
         self.y_chan = [lax.rem(self.y + dy, 4) * 4 for dy in range(4)]
 
     def away(self, dx, dy, dz, dcore):

time: 62.3 us -> 62.3 us (level)
  no operation moved by 1% of the time
where the time goes in v7:
time: 62.3 us
  Pallas kernels  62.3 us (100%)
    pallas_call x1, Pallas kernels, spectra_of(): pl.pallas_call(spectra_kernel, out_shape=(jax.ShapeDtypeStruct((INPUTS, I...  58.9 us
    pallas_call x1, Pallas kernels, gram(): pl.pallas_call(gram_kernel, out_shape=jax.ShapeDtypeStruct((2, INPUTS, IN...  3.35 us

profile of v7, /device:TPU:33, one launch (start us, length us, event | category | flops | bytes accessed | tf_op | source)
XLA Modules:
  0.0 62.3 jit_solution(2296618254377836146)
XLA Ops:
  0.0 58.9 %spectra_exchange.1 = (f32[1024,1024]{1,0:T(8,128)S(1)}, bf16[1024,512]{1,0:T(8,128)(2,1)S(1)}) custom-call(bf16[259,64,128]{2,1,0:T(8,128)(2,1)} %bitcast.5, f32[192,64,128]{2,1,0:T(8,128)} %constant.4.clone.window_hbm, bf16[4,256,2048]{2,1,0:T(8,128)(2,1)} %constant.5.clone.table_hbm), custom_call_target="tpu_custom_call" | custom-call | tf_op jit(solution)/shard_map/spectra_exchange/pallas_call | solution.py:285
  58.9 3.4 %gram.1 = f32[2,1024,1024]{2,1,0:T(8,128)} custom-call(f32[1024,1024]{1,0:T(8,128)S(1)} %get-tuple-element.7.first_ref, bf16[1024,512]{1,0:T(8,128)(2,1)S(1)} %get-tuple-element.8.in_ref), custom_call_target="tpu_custom_call" | custom-call | tf_op jit(solution)/shard_map/gram/pallas_call | solution.py:337
